TPU v7x, 32 devices: a whole 2x2x4 slice. The times are simulated.
32 devices in a mesh: doc: 8 (over z, y), head: 4 (over x, core).
Axes of the slice: x: 2, y: 2, z: 4, core: 2. Of those that a mesh axis runs over, the one named last changes fastest.
Arguments:
- target_q: bfloat16 [1024, 2048], P('doc', 'head'), may hold values from -300 to 300
- target_kv: bfloat16 [1024, 512], P('doc', 'head'), may hold values from -8 to 8
- doc_kv: bfloat16 [8, 384, 512], P('doc', None, 'head'), may hold values from -6 to 6
- doc_lengths: int32 [8], replicated, may hold values from 1 to 384, 2304 in all
- segment_ids: int32 [1024], replicated, may hold values from 0 to 15, never falling along the last dimension, each value on 1 to 128 neighbouring positions
- out_weight: bfloat16 [2048, 8192], P('head', 'doc'), may hold values from -0.125 to 0.125
Outputs:
- projected: bfloat16 [1024, 8192], P('head', 'doc')
Inputs may be any that keep to these rules, and one draw needn't show every extreme that they name: `segment_ids`: segment numbers never fall along the target rows, and each segment spans at most 128 rows.
All inputs are finite; a program needn't handle non-finite values.
Results may differ from a plain program's by a relative error of at most 0.005.
Values may be sent and summed in bfloat16 or wider, within the bound.
A program may use at most 64 MiB of HBM per device.

v0:
```python
import math
import jax
import jax.numpy as jnp
from jax import lax
from jax.sharding import PartitionSpec as P

masked_score = -1e30


def swapped(array, axis, stride):
    return lax.ppermute(array, axis, [(i, i ^ 1 << stride) for i in range(lax.axis_size(axis))])


def passed_along(value, axis, steps):
    count = lax.axis_size(axis)
    initial, last = (max(0, -steps), min(count, count - steps))
    return lax.ppermute(value, axis, [(source, source + steps) for source in range(initial, last)])


def block_stats(queries, key_block, value_block, visible):
    scaling = 1.0 / math.sqrt(key_block.shape[1])
    scores = (
        lax.dot_general(
            queries, key_block, (((1,), (1,)), ((), ())), preferred_element_type=jnp.float32
        )
        * scaling
    )
    scores = jnp.where(visible, scores, masked_score)
    highest = jnp.max(scores, axis=1)
    weights = jnp.exp(scores - highest[:, None])
    summed = jnp.sum(weights, axis=1)
    blended = jnp.dot(weights.astype(jnp.bfloat16), value_block, preferred_element_type=jnp.float32)
    return (highest, summed, blended)


def merge_stats(state_now, incoming):
    highest = jnp.maximum(state_now[0], incoming[0])
    old_factor = jnp.exp(state_now[0] - highest)
    new_factor = jnp.exp(incoming[0] - highest)
    summed = state_now[1] * old_factor + incoming[1] * new_factor
    blended = state_now[2] * old_factor[:, None] + incoming[2] * new_factor[:, None]
    return (highest, summed, blended)


def body(target_q, target_kv, doc_kv, doc_lengths, segment_ids, out_weight):
    row_count = target_q.shape[0]
    head_dim = target_kv.shape[1]
    per_device = target_q.shape[1] // head_dim
    queries = target_q.reshape(row_count * per_device, head_dim)
    parity = lax.axis_index("head") % 2
    doc_index = lax.axis_index("doc")

    def arrange(own_part, partner):
        return (
            jnp.where(parity == 0, own_part, partner),
            jnp.where(parity == 0, partner, own_part),
        )

    initial = (
        jnp.full((queries.shape[0],), masked_score, jnp.float32),
        jnp.zeros((queries.shape[0],), jnp.float32),
        jnp.zeros((queries.shape[0], head_dim), jnp.float32),
    )
    partner_doc, partner_tgt = swapped((doc_kv, target_kv), "head", 0)
    doc_keys, doc_values = arrange(doc_kv, partner_doc)
    key_docs = lax.all_gather(doc_keys, "doc", axis=0, tiled=True)
    value_docs = lax.all_gather(doc_values, "doc", axis=0, tiled=True)
    slot_index = jnp.arange(key_docs.shape[1], dtype=jnp.int32)

    def attend_doc(doc_step, running):
        key_block = lax.dynamic_index_in_dim(key_docs, doc_step, 0, keepdims=False)
        value_block = lax.dynamic_index_in_dim(value_docs, doc_step, 0, keepdims=False)
        length = lax.dynamic_index_in_dim(doc_lengths, doc_step, 0, keepdims=False)
        visible = (slot_index < length)[None, :]
        return merge_stats(running, block_stats(queries, key_block, value_block, visible))

    stats = lax.fori_loop(0, key_docs.shape[0], attend_doc, initial)
    own_keys, own_values = arrange(target_kv, partner_tgt)
    prev_keys, prev_values = passed_along((own_keys, own_values), "doc", 1)
    own_seg = lax.dynamic_slice_in_dim(segment_ids, doc_index * row_count, row_count)
    prev_start = jnp.maximum(doc_index - 1, 0) * row_count
    prev_seg = jnp.where(
        doc_index > 0, lax.dynamic_slice_in_dim(segment_ids, prev_start, row_count), -1
    )
    token_pos = jnp.arange(row_count, dtype=jnp.int32)
    own_mask = (own_seg[:, None] == own_seg[None, :]) & (token_pos[None, :] <= token_pos[:, None])
    prev_mask = own_seg[:, None] == prev_seg[None, :]
    stats = merge_stats(
        stats, block_stats(queries, own_keys, own_values, jnp.repeat(own_mask, per_device, axis=0))
    )
    stats = merge_stats(
        stats,
        block_stats(queries, prev_keys, prev_values, jnp.repeat(prev_mask, per_device, axis=0)),
    )
    attention = (
        (stats[2] / stats[1][:, None])
        .astype(jnp.bfloat16)
        .reshape(row_count, per_device * head_dim)
    )
    gathered = lax.all_gather(attention, "doc", axis=0, tiled=True)
    result = lax.psum_scatter(
        jnp.dot(gathered, out_weight, preferred_element_type=jnp.float32),
        "head",
        scatter_dimension=0,
        tiled=True,
    )
    return result.astype(jnp.bfloat16)


def solution(mesh):
    placed = (
        P("doc", "head"),
        P("doc", "head"),
        P("doc", None, "head"),
        P(),
        P(),
        P("head", "doc"),
    )
    return jax.shard_map(
        body, mesh=mesh, in_specs=placed, out_specs=P("head", "doc"), check_vma=False
    )
```

profile of v0, /device:TPU:0, one launch (start us, length us, event | category | flops | bytes accessed | tf_op | source)
XLA Modules:
  0.0 207.3 jit_solution(15352952914273228183)
XLA Ops:
  6.5 0.5 collective-permute-start.1
  7.1 0.8 fusion.38
  8.1 0.1 copy.9
  8.3 0.1 copy.10
  8.5 1.0 reshape.30
  9.5 1.4 broadcast_select_fusion.3
  10.9 4.9 %collective-permute-start.2 = (bf16[128,128]{1,0:T(8,128)(2,1)S(1)}, bf16[128,128]{1,0:T(8,128)(2,1)S(1)}, u32[]{:S(2)}, u32[]{:S(2)}) collective-permute-start(bf16[128,128]{1,0:T(8,128)(2,1)S(1)} %get-tuple-element.222), channel_id=1, source_target_pairs={{0,4},{4,8},{8,12},{12,16},{16,20},{20,24},{24,28},{1,5},{5,9},{9,... | collective-permute-start | bytes 98312 | tf_op jit(solution)/shard_map/ppermute | solution.py:17
  15.7 4.0 %collective-permute-start.3 = (bf16[128,128]{1,0:T(8,128)(2,1)}, bf16[128,128]{1,0:T(8,128)(2,1)}, u32[]{:S(2)}, u32[]{:S(2)}) collective-permute-start(bf16[128,128]{1,0:T(8,128)(2,1)} %get-tuple-element.223), channel_id=1, source_target_pairs={{0,4},{4,8},{8,12},{12,16},{16,20},{20,24},{24,28},{1,5},{5,9},{9,... | collective-permute-start | bytes 98312 | tf_op jit(solution)/shard_map/ppermute | solution.py:17
  19.8 0.2 fusion.40
  20.0 0.6 fusion.24
  20.6 0.2 fusion.39
  20.8 0.6 fusion.26
  21.5 0.9 broadcast_select_fusion
  22.4 32.1 %all_gather.10 = bf16[8,384,128]{2,1,0:T(8,128)(2,1)S(1)} all-gather(bf16[1,384,128]{2,1,0:T(8,128)(2,1)S(1)} %get-tuple-element.220), channel_id=1, replica_groups=mesh['doc'=8,'head'=4] {'doc'}, dimensions={0}, use_global_device_ids=true | all-gather | bytes 884736 | tf_op jit(solution)/shard_map/all_gather | solution.py:67
  54.5 32.1 %all_gather.9 = bf16[8,384,128]{2,1,0:T(8,128)(2,1)S(1)} all-gather(bf16[1,384,128]{2,1,0:T(8,128)(2,1)S(1)} %get-tuple-element.221), channel_id=1, replica_groups=mesh['doc'=8,'head'=4] {'doc'}, dimensions={0}, use_global_device_ids=true | all-gather | bytes 884736 | tf_op jit(solution)/shard_map/all_gather | solution.py:66
  86.7 21.7 %while.18 = (s32[]{:T(128)}, f32[512]{0:T(512)S(1)}, f32[512]{0:T(512)S(1)}, f32[512,128]{1,0:T(8,128)S(1)}, s32[8]{0:T(128)}, /*index=5*/bf16[8,384,128]{2,1,0:...) while((s32[]{:T(128)}, f32[512]{0:T(512)S(1)}, ...), condition=%wide.region_3.4_spmd.clone, body=%wide.region_0.3_spmd.clone.sunk | while | flops 102305152 | bytes 3240976 | solution.py:77
  86.7 1.2 dynamic_slice.51
  87.9 0.6 iota_compare_fusion.3
  88.5 0.3 fusion.61
  88.8 0.2 fusion.62
  88.9 0.4 fusion.64
  89.4 1.2 dynamic_slice.51
  90.6 0.6 iota_compare_fusion.3
  91.2 0.3 fusion.61
  91.5 0.2 fusion.62
  91.6 0.4 fusion.64
  92.1 1.2 dynamic_slice.51
  93.3 0.6 iota_compare_fusion.3
  93.9 0.3 fusion.61
  94.2 0.2 fusion.62
  94.3 0.4 fusion.64
  94.8 1.2 dynamic_slice.51
  96.0 0.6 iota_compare_fusion.3
  96.6 0.3 fusion.61
  96.9 0.2 fusion.62
  97.1 0.4 fusion.64
  97.5 1.2 dynamic_slice.51
  98.7 0.6 iota_compare_fusion.3
  99.3 0.3 fusion.61
  99.6 0.2 fusion.62
  99.8 0.4 fusion.64
  100.2 1.2 dynamic_slice.51
  101.4 0.6 iota_compare_fusion.3
  102.0 0.3 fusion.61
  102.3 0.2 fusion.62
  102.5 0.4 fusion.64
  102.9 1.2 dynamic_slice.51
  104.2 0.6 iota_compare_fusion.3
  104.7 0.3 fusion.61
  105.0 0.2 fusion.62
  105.2 0.4 fusion.64
  105.6 1.2 dynamic_slice.51
  106.9 0.6 iota_compare_fusion.3
  107.4 0.3 fusion.61
  107.7 0.2 fusion.62
  107.9 0.4 fusion.64
  108.3 0.7 multiply_add_fusion
  109.0 1.0 convolution_multiply_fusion.2
  110.0 1.2 fusion.23
  111.2 0.7 reshape.33
  112.0 38.6 %all-gather.2.cloned.1.call-done = bf16[1024,512]{1,0:T(8,128)(2,1)} async-done(((bf16[128,512]{1,0:T(8,128)(2,1)}), bf16[1024,512]{1,0:T(8,128)(2,1)}) %all-gather.2.cloned.1.call-update) | async-done | bytes 1048592 | tf_op jit(solution)/shard_map/all_gather | solution.py:100
  150.6 4.4 %fusion.41 = f32[1024,1024]{1,0:T(8,128)} fusion(bf16[1024,512]{1,0:T(8,128)(2,1)} %all-gather.2.cloned.1.call-done, bf16[512,1024]{1,0:T(8,128)(2,1)S(1)} %copy-done), kind=kOutput, calls=%fused_computation.62 | convolution fusion | flops 1073741824 | bytes 6291456 | tf_op jit(solution)/shard_map/dot_general | solution.py:102
  155.0 43.4 %reduce-scatter.2.cloned.1.call-done = f32[256,1024]{1,0:T(8,128)} async-done(((f32[1024,1024]{1,0:T(8,128)}), f32[256,1024]{1,0:T(8,128)}) %reduce-scatter.2.cloned.1.call-update) | async-done | bytes 1048592 | tf_op jit(solution)/shard_map/reduce_scatter | solution.py:101
  198.4 2.1 %convert_element_type.20 = bf16[256,1024]{1,0:T(8,128)(2,1)} convert(f32[256,1024]{1,0:T(8,128)} %reduce-scatter.2.cloned.1.call-done) | non-fusion elementwise | flops 262144 | bytes 1572864 | tf_op jit(solution)/shard_map/convert_element_type | solution.py:107
  (25 shorter events, 0.5 us)
Async XLA Ops:
  6.5 144.0 %copy-start = (bf16[512,1024]{1,0:T(8,128)(2,1)S(1)}, bf16[512,1024]{1,0:T(8,128)(2,1)}, u32[]{:S(2)}) copy-start(bf16[512,1024]{1,0:T(8,128)(2,1)} %param.13) | copy-start | bytes 3145732
  6.5 144.0 %all-gather.2.cloned.1.call-start = ((), (), s32[]{:S(2)}) async-start(), calls=%async_computation.1 | async-start | bytes 1179648 | tf_op jit(solution)/shard_map/all_gather | solution.py:100
  6.5 2.9 %collective-permute-start.1 = (bf16[128,128]{1,0:T(8,128)(2,1)}, bf16[128,128]{1,0:T(8,128)(2,1)S(1)}, u32[]{:S(2)}, u32[]{:S(2)}) collective-permute-start(bf16[128,128]{1,0:T(8,128)(2,1)} %param.9), channel_id=1, source_target_pairs={{0,1},{1,0},{2,3},{3,2},{4,5},{5,4},{6,7},{7,6},{8,9},{9,8},{10,11... | collective-permute-start | bytes 98312 | tf_op jit(solution)/shard_map/ppermute | solution.py:11
  7.0 14.5 %collective-permute-start = (bf16[1,384,128]{2,1,0:T(8,128)(2,1)}, bf16[1,384,128]{2,1,0:T(8,128)(2,1)S(1)}, u32[]{:S(2)}, u32[]{:S(2)}) collective-permute-start(bf16[1,384,128]{2,1,0:T(8,128)(2,1)} %param.10), channel_id=1, source_target_pairs={{0,1},{1,0},{2,3},{3,2},{4,5},{5,4},{6,7},{7,6},{8,9},{9,8},{10,11... | collective-permute-start | bytes 294920 | tf_op jit(solution)/shard_map/ppermute | solution.py:11
  10.9 9.8 %collective-permute-start.2 = (bf16[128,128]{1,0:T(8,128)(2,1)S(1)}, bf16[128,128]{1,0:T(8,128)(2,1)S(1)}, u32[]{:S(2)}, u32[]{:S(2)}) collective-permute-start(bf16[128,128]{1,0:T(8,128)(2,1)S(1)} %get-tuple-element.222), channel_id=1, source_target_pairs={{0,4},{4,8},{8,12},{12,16},{16,20},{20,24},{24,28},{1,5},{5,9},{9,... | collective-permute-start | bytes 98312 | tf_op jit(solution)/shard_map/ppermute | solution.py:17
  15.7 93.3 %collective-permute-start.3 = (bf16[128,128]{1,0:T(8,128)(2,1)}, bf16[128,128]{1,0:T(8,128)(2,1)}, u32[]{:S(2)}, u32[]{:S(2)}) collective-permute-start(bf16[128,128]{1,0:T(8,128)(2,1)} %get-tuple-element.223), channel_id=1, source_target_pairs={{0,4},{4,8},{8,12},{12,16},{16,20},{20,24},{24,28},{1,5},{5,9},{9,... | collective-permute-start | bytes 98312 | tf_op jit(solution)/shard_map/ppermute | solution.py:17
  111.9 86.5 %reduce-scatter.2.cloned.1.call-start = ((), (), s32[]{:S(2)}) async-start(), calls=%async_computation.2 | async-start | bytes 5242880 | tf_op jit(solution)/shard_map/reduce_scatter | solution.py:101
Sparse Core Ops, SparseCore 0:
  112.1 38.4 all-gather.1
  155.1 43.2 reduce-scatter.1
where the time goes:
time: 208 us; the launch traced here: 207 us
  waiting for transfers between devices  82 us (39%)
  blocking collectives  64.3 us (31%)
  between operations  13.6 us (7%)
  other arithmetic  13.1 us (6%)
  matrix products  12.6 us (6%)
  local copies, waits for them, and re-layouts  12 us (6%)
  starting transfers between devices  9.46 us (5%)
    reduce_scatter x1, waiting for transfers between devices, body(): lax.psum_scatter(jnp.dot(gathered, out_weight, preferred_element_type=jnp...  43.4 us
    all_gather x1, waiting for transfers between devices, body(): gathered = lax.all_gather(attention, 'doc', axis=0, tiled=True)  38.6 us
    all_gather x1, blocking collectives, body(): key_docs = lax.all_gather(doc_keys, 'doc', axis=0, tiled=True)  32.1 us
    all_gather x1, blocking collectives, body(): value_docs = lax.all_gather(doc_values, 'doc', axis=0, tiled=True)  32.1 us
    dynamic_slice x8, local copies, waits for them, and re-layouts, attend_doc(): length = lax.dynamic_index_in_dim(doc_lengths, doc_step, 0, keepdims=False)  9.87 us
    ppermute x2, starting transfers between devices, passed_along(): lax.ppermute(value, axis, [(source, source + steps) for source in range(i...  8.91 us
    dot_general x10, matrix products, block_stats(): jnp.dot(weights.astype(jnp.bfloat16), value_block, preferred_element_type...  5.52 us
    lt x8, other arithmetic, attend_doc(): visible = (slot_index < length)[None, :]  4.5 us
  transfers between devices with their start and end apart: 6, of which 2 were waited for; matrix products, arithmetic and copies ran while one was open for 14% of the time, Pallas kernels for 0%

commit v1 on v0

--- a/solution.py
+++ b/solution.py
@@ -1,3 +1,4 @@
+import functools
 import math
 import jax
 import jax.numpy as jnp
@@ -5,6 +6,21 @@
 from jax.sharding import PartitionSpec as P
 
 masked_score = -1e30
+
+
+def members_all_arrange(target, net_axis):
+    parts_n = lax.psum(1, net_axis)
+    part_next = [None] * parts_n
+    part_next[parts_n - 1] = target
+    pile = [(k, (k + 1) % parts_n) for k in range(parts_n)]
+    for dd in range(parts_n - 2, -1, -1):
+        part_next[dd] = lax.ppermute(part_next[dd + 1], net_axis, pile)
+    return jnp.roll(
+        jnp.concatenate(part_next, axis=0), (lax.axis_index(net_axis) + 1) * target.shape[0], axis=0
+    )
+
+
+_solve_inputs = functools.partial(members_all_arrange, net_axis="doc")
 
 
 def swapped(array, axis, stride):
@@ -64,7 +80,7 @@
     partner_doc, partner_tgt = swapped((doc_kv, target_kv), "head", 0)
     doc_keys, doc_values = arrange(doc_kv, partner_doc)
     key_docs = lax.all_gather(doc_keys, "doc", axis=0, tiled=True)
-    value_docs = lax.all_gather(doc_values, "doc", axis=0, tiled=True)
+    value_docs = _solve_inputs(doc_values)
     slot_index = jnp.arange(key_docs.shape[1], dtype=jnp.int32)
 
     def attend_doc(doc_step, running):

time: 208 us -> 221 us (1.062)
  waiting for transfers between devices: 82 us -> 116 us
  blocking collectives: 64.3 us -> 32.8 us
  matrix products: 12.6 us -> 19.8 us
    all_gather x1 -> x0, blocking collectives: 32.1 us -> none  [body(): value_docs = lax.all_gather(doc_values, 'doc', axis=0, tiled=True)]
    ppermute x0 -> x7, waiting for transfers between devices: none -> 31 us  [members_all_arrange(): part_next[dd] = lax.ppermute(part_next[dd + 1], net_axis, pile)]
    dot_general x10, matrix products: 5.52 us -> 12.7 us  [block_stats(): jnp.dot(weights.astype(jnp.bfloat16), value_block, preferred_element_type...]
    ppermute x0 -> x7, starting transfers between devices: none -> 4.83 us  [members_all_arrange(): part_next[dd] = lax.ppermute(part_next[dd + 1], net_axis, pile)]
    ppermute x2, starting transfers between devices: 8.91 us -> 6.14 us  [passed_along(): lax.ppermute(value, axis, [(source, source + steps) for source in range(i...]
    all_gather x1, waiting for transfers between devices: 38.6 us -> 41.1 us  [body(): gathered = lax.all_gather(attention, 'doc', axis=0, tiled=True)]
  transfers between devices with their start and end apart: 6 -> 13, of which waited for: 2 -> 8; matrix products, arithmetic and copies ran while one was open for 14% -> 17% of each run, Pallas kernels for 0% -> 0%
where the time goes in v1:
time: 221 us; the launch traced here: 220 us
  waiting for transfers between devices  116 us (52%)
  blocking collectives  32.8 us (15%)
  matrix products  19.8 us (9%)
  between operations  13.7 us (6%)
  local copies, waits for them, and re-layouts  13.3 us (6%)
  other arithmetic  13.2 us (6%)
  starting transfers between devices  11.5 us (5%)
    reduce_scatter x1, waiting for transfers between devices, body(): lax.psum_scatter(jnp.dot(gathered, out_weight, preferred_element_type=jnp...  43.4 us
    all_gather x1, waiting for transfers between devices, body(): gathered = lax.all_gather(attention, 'doc', axis=0, tiled=True)  41.1 us
    all_gather x1, blocking collectives, body(): key_docs = lax.all_gather(doc_keys, 'doc', axis=0, tiled=True)  32.8 us
    ppermute x7, waiting for transfers between devices, members_all_arrange(): part_next[dd] = lax.ppermute(part_next[dd + 1], net_axis, pile)  31 us
    dot_general x10, matrix products, block_stats(): jnp.dot(weights.astype(jnp.bfloat16), value_block, preferred_element_type...  12.7 us
    dynamic_slice x8, local copies, waits for them, and re-layouts, attend_doc(): length = lax.dynamic_index_in_dim(doc_lengths, doc_step, 0, keepdims=False)  9.93 us
    ppermute x2, starting transfers between devices, passed_along(): lax.ppermute(value, axis, [(source, source + steps) for source in range(i...  6.14 us
    ppermute x7, starting transfers between devices, members_all_arrange(): part_next[dd] = lax.ppermute(part_next[dd + 1], net_axis, pile)  4.83 us
  transfers between devices with their start and end apart: 13, of which 8 were waited for; matrix products, arithmetic and copies ran while one was open for 17% of the time, Pallas kernels for 0%

profile of v1, /device:TPU:0, one launch (start us, length us, event | category | flops | bytes accessed | tf_op | source)
XLA Modules:
  0.0 220.3 jit_solution(2083544164685528893)
XLA Ops:
  6.5 0.5 collective-permute-start
  7.1 0.8 fusion.38
  7.9 0.3 collective-permute-done
  8.1 0.9 broadcast_select_fusion
  9.1 2.9 %collective-permute-start.1 = (bf16[1,384,128]{2,1,0:T(8,128)(2,1)S(1)}, bf16[1,384,128]{2,1,0:T(8,128)(2,1)S(1)}, u32[]{:S(2)}, u32[]{:S(2)}) collective-permute-start(bf16[1,384,128]{2,1,0:T(8,128)(2,1)S(1)} %get-tuple-element.220), channel_id=1, source_target_pairs={{0,4},{4,8},{8,12},{12,16},{16,20},{20,24},{24,28},{28,0},{1,5},{5... | collective-permute-start | bytes 294920 | tf_op jit(solution)/shard_map/ppermute | solution.py:17
  12.1 1.0 reshape.30
  13.6 4.6 %collective-permute-done.1 = bf16[1,384,128]{2,1,0:T(8,128)(2,1)S(1)} collective-permute-done((bf16[1,384,128]{2,1,0:T(8,128)(2,1)S(1)}, bf16[1,384,128]{2,1,0:T(8,128)(2,1)S(1)}, u32[]{:S(2)}, u32[]{:S(2)}) %collective-permute-start.1) | collective-permute-done | bytes 98336 | tf_op jit(solution)/shard_map/ppermute | solution.py:17
  18.1 1.4 broadcast_select_fusion.3
  19.5 3.0 %collective-permute-start.9 = (bf16[128,128]{1,0:T(8,128)(2,1)S(1)}, bf16[128,128]{1,0:T(8,128)(2,1)S(1)}, u32[]{:S(2)}, u32[]{:S(2)}) collective-permute-start(bf16[128,128]{1,0:T(8,128)(2,1)S(1)} %get-tuple-element.222), channel_id=1, source_target_pairs={{0,4},{4,8},{8,12},{12,16},{16,20},{20,24},{24,28},{1,5},{5,9},{9,... | collective-permute-start | bytes 98312 | tf_op jit(solution)/shard_map/ppermute | solution.py:33
  22.5 3.1 %collective-permute-start.10 = (bf16[128,128]{1,0:T(8,128)(2,1)}, bf16[128,128]{1,0:T(8,128)(2,1)}, u32[]{:S(2)}, u32[]{:S(2)}) collective-permute-start(bf16[128,128]{1,0:T(8,128)(2,1)} %get-tuple-element.223), channel_id=1, source_target_pairs={{0,4},{4,8},{8,12},{12,16},{16,20},{20,24},{24,28},{1,5},{5,9},{9,... | collective-permute-start | bytes 98312 | tf_op jit(solution)/shard_map/ppermute | solution.py:33
  25.7 1.9 collective-permute-start.3
  27.6 0.2 fusion.40
  27.8 5.2 %collective-permute-done.3 = bf16[1,384,128]{2,1,0:T(8,128)(2,1)S(1)} collective-permute-done((bf16[1,384,128]{2,1,0:T(8,128)(2,1)S(1)}, bf16[1,384,128]{2,1,0:T(8,128)(2,1)S(1)}, u32[]{:S(2)}, u32[]{:S(2)}) %collective-permute-start.3) | collective-permute-done | bytes 98336 | tf_op jit(solution)/shard_map/ppermute | solution.py:17
  33.0 0.6 fusion.24
  33.6 6.7 %collective-permute-done.4 = bf16[1,384,128]{2,1,0:T(8,128)(2,1)S(1)} collective-permute-done((bf16[1,384,128]{2,1,0:T(8,128)(2,1)S(1)}, bf16[1,384,128]{2,1,0:T(8,128)(2,1)S(1)}, u32[]{:S(2)}, u32[]{:S(2)}) %collective-permute-start.4) | collective-permute-done | bytes 98336 | tf_op jit(solution)/shard_map/ppermute | solution.py:17
  40.3 0.2 fusion.39
  40.5 7.1 %collective-permute-done.5 = bf16[1,384,128]{2,1,0:T(8,128)(2,1)S(1)} collective-permute-done((bf16[1,384,128]{2,1,0:T(8,128)(2,1)S(1)}, bf16[1,384,128]{2,1,0:T(8,128)(2,1)S(1)}, u32[]{:S(2)}, u32[]{:S(2)}) %collective-permute-start.5) | collective-permute-done | bytes 98336 | tf_op jit(solution)/shard_map/ppermute | solution.py:17
  47.6 0.7 fusion.26
  48.3 7.5 %collective-permute-done.6 = bf16[1,384,128]{2,1,0:T(8,128)(2,1)S(1)} collective-permute-done((bf16[1,384,128]{2,1,0:T(8,128)(2,1)S(1)}, bf16[1,384,128]{2,1,0:T(8,128)(2,1)S(1)}, u32[]{:S(2)}, u32[]{:S(2)}) %collective-permute-start.6) | collective-permute-done | bytes 98336 | tf_op jit(solution)/shard_map/ppermute | solution.py:17
  55.8 32.8 %all_gather.6 = bf16[8,384,128]{2,1,0:T(8,128)(2,1)S(1)} all-gather(bf16[1,384,128]{2,1,0:T(8,128)(2,1)S(1)} %get-tuple-element.221), channel_id=1, replica_groups=mesh['doc'=8,'head'=4] {'doc'}, dimensions={0}, use_global_device_ids=true | all-gather | bytes 884736 | tf_op jit(solution)/shard_map/all_gather | solution.py:82
  88.9 0.9 constant_dynamic-slice_fusion
  89.9 28.8 %while.18 = (s32[]{:T(128)}, f32[512]{0:T(512)S(1)}, f32[512]{0:T(512)S(1)}, f32[512,128]{1,0:T(8,128)S(1)}, s32[8]{0:T(128)}, /*index=5*/bf16[8,384,128]{2,1,0:...) while((s32[]{:T(128)}, f32[512]{0:T(512)S(1)}, ...), condition=%wide.region_3.4_spmd.clone, body=%wide.region_0.3_spmd.clone.sunk | while | flops 102305152 | bytes 3241476 | solution.py:93
  89.9 1.2 dynamic_slice.57
  91.1 0.6 iota_compare_fusion.3
  91.7 0.3 fusion.61
  92.1 1.3 fusion.64
  93.5 1.2 dynamic_slice.57
  94.7 0.6 iota_compare_fusion.3
  95.3 0.3 fusion.61
  95.7 1.3 fusion.64
  97.1 1.2 dynamic_slice.57
  98.3 0.6 iota_compare_fusion.3
  98.9 0.3 fusion.61
  99.3 1.3 fusion.64
  100.7 1.2 dynamic_slice.57
  101.9 0.6 iota_compare_fusion.3
  102.5 0.3 fusion.61
  102.9 1.3 fusion.64
  104.3 1.2 dynamic_slice.57
  105.5 0.6 iota_compare_fusion.3
  106.1 0.3 fusion.61
  106.6 1.3 fusion.64
  107.9 1.2 dynamic_slice.57
  109.1 0.6 iota_compare_fusion.3
  109.7 0.3 fusion.61
  110.0 0.2 fusion.62
  110.2 1.3 fusion.64
  111.5 1.2 dynamic_slice.57
  112.7 0.6 iota_compare_fusion.3
  113.3 0.3 fusion.61
  113.6 0.2 fusion.62
  113.8 1.3 fusion.64
  115.1 1.2 dynamic_slice.57
  116.3 0.6 iota_compare_fusion.3
  116.9 0.3 fusion.61
  117.4 1.3 fusion.64
  118.7 0.7 multiply_add_fusion
  119.4 1.0 convolution_multiply_fusion.2
  120.4 1.2 fusion.23
  121.6 0.7 reshape.33
  122.4 41.1 %all-gather.2.cloned.1.call-done = bf16[1024,512]{1,0:T(8,128)(2,1)} async-done(((bf16[128,512]{1,0:T(8,128)(2,1)}), bf16[1024,512]{1,0:T(8,128)(2,1)}) %all-gather.2.cloned.1.call-update) | async-done | bytes 1048592 | tf_op jit(solution)/shard_map/all_gather | solution.py:116
  163.5 4.4 %fusion.41 = f32[1024,1024]{1,0:T(8,128)} fusion(bf16[1024,512]{1,0:T(8,128)(2,1)} %all-gather.2.cloned.1.call-done, bf16[512,1024]{1,0:T(8,128)(2,1)S(1)} %copy-done), kind=kOutput, calls=%fused_computation.79 | convolution fusion | flops 1073741824 | bytes 6291456 | tf_op jit(solution)/shard_map/dot_general | solution.py:118
  168.0 43.4 %reduce-scatter.2.cloned.1.call-done = f32[256,1024]{1,0:T(8,128)} async-done(((f32[1024,1024]{1,0:T(8,128)}), f32[256,1024]{1,0:T(8,128)}) %reduce-scatter.2.cloned.1.call-update) | async-done | bytes 1048592 | tf_op jit(solution)/shard_map/reduce_scatter | solution.py:117
  211.4 2.1 convert_element_type.20
  (59 shorter events, 2.0 us)
Async XLA Ops:
  6.5 157.0 %copy-start = (bf16[512,1024]{1,0:T(8,128)(2,1)S(1)}, bf16[512,1024]{1,0:T(8,128)(2,1)}, u32[]{:S(2)}) copy-start(bf16[512,1024]{1,0:T(8,128)(2,1)} %param.13) | copy-start | bytes 3145732
  6.5 157.0 %all-gather.2.cloned.1.call-start = ((), (), s32[]{:S(2)}) async-start(), calls=%async_computation.1 | async-start | bytes 1179648 | tf_op jit(solution)/shard_map/all_gather | solution.py:116
  6.5 1.6 collective-permute-start
  7.0 11.1 %collective-permute-start.8 = (bf16[128,128]{1,0:T(8,128)(2,1)}, bf16[128,128]{1,0:T(8,128)(2,1)S(1)}, u32[]{:S(2)}, u32[]{:S(2)}) collective-permute-start(bf16[128,128]{1,0:T(8,128)(2,1)} %param.9), channel_id=1, source_target_pairs={{0,1},{1,0},{2,3},{3,2},{4,5},{5,4},{6,7},{7,6},{8,9},{9,8},{10,11... | collective-permute-start | bytes 98312 | tf_op jit(solution)/shard_map/ppermute | solution.py:27
  9.1 9.1 %collective-permute-start.1 = (bf16[1,384,128]{2,1,0:T(8,128)(2,1)S(1)}, bf16[1,384,128]{2,1,0:T(8,128)(2,1)S(1)}, u32[]{:S(2)}, u32[]{:S(2)}) collective-permute-start(bf16[1,384,128]{2,1,0:T(8,128)(2,1)S(1)} %get-tuple-element.220), channel_id=1, source_target_pairs={{0,4},{4,8},{8,12},{12,16},{16,20},{20,24},{24,28},{28,0},{1,5},{5... | collective-permute-start | bytes 294920 | tf_op jit(solution)/shard_map/ppermute | solution.py:17
  18.1 7.5 %collective-permute-start.2 = (bf16[1,384,128]{2,1,0:T(8,128)(2,1)S(1)}, bf16[1,384,128]{2,1,0:T(8,128)(2,1)S(1)}, u32[]{:S(2)}, u32[]{:S(2)}) collective-permute-start(bf16[1,384,128]{2,1,0:T(8,128)(2,1)S(1)} %collective-permute-done.1), channel_id=1, source_target_pairs={{0,4},{4,8},{8,12},{12,16},{16,20},{20,24},{24,28},{28,0},{1,5},{5... | collective-permute-start | bytes 294920 | tf_op jit(solution)/shard_map/ppermute | solution.py:17
  19.5 20.8 %collective-permute-start.9 = (bf16[128,128]{1,0:T(8,128)(2,1)S(1)}, bf16[128,128]{1,0:T(8,128)(2,1)S(1)}, u32[]{:S(2)}, u32[]{:S(2)}) collective-permute-start(bf16[128,128]{1,0:T(8,128)(2,1)S(1)} %get-tuple-element.222), channel_id=1, source_target_pairs={{0,4},{4,8},{8,12},{12,16},{16,20},{20,24},{24,28},{1,5},{5,9},{9,... | collective-permute-start | bytes 98312 | tf_op jit(solution)/shard_map/ppermute | solution.py:33
  22.5 96.9 %collective-permute-start.10 = (bf16[128,128]{1,0:T(8,128)(2,1)}, bf16[128,128]{1,0:T(8,128)(2,1)}, u32[]{:S(2)}, u32[]{:S(2)}) collective-permute-start(bf16[128,128]{1,0:T(8,128)(2,1)} %get-tuple-element.223), channel_id=1, source_target_pairs={{0,4},{4,8},{8,12},{12,16},{16,20},{20,24},{24,28},{1,5},{5,9},{9,... | collective-permute-start | bytes 98312 | tf_op jit(solution)/shard_map/ppermute | solution.py:33
  25.7 7.3 %collective-permute-start.3 = (bf16[1,384,128]{2,1,0:T(8,128)(2,1)S(1)}, bf16[1,384,128]{2,1,0:T(8,128)(2,1)S(1)}, u32[]{:S(2)}, u32[]{:S(2)}) collective-permute-start(bf16[1,384,128]{2,1,0:T(8,128)(2,1)S(1)} %collective-permute-done.2), channel_id=1, source_target_pairs={{0,4},{4,8},{8,12},{12,16},{16,20},{20,24},{24,28},{28,0},{1,5},{5... | collective-permute-start | bytes 294920 | tf_op jit(solution)/shard_map/ppermute | solution.py:17
  27.8 12.5 %copy-start.2 = (f32[512]{0:T(512)}, f32[512]{0:T(512)S(1)}, u32[]{:S(2)}) copy-start(f32[512]{0:T(512)S(1)} %get-tuple-element.230) | copy-start | bytes 6148
  33.0 7.3 %collective-permute-start.4 = (bf16[1,384,128]{2,1,0:T(8,128)(2,1)S(1)}, bf16[1,384,128]{2,1,0:T(8,128)(2,1)S(1)}, u32[]{:S(2)}, u32[]{:S(2)}) collective-permute-start(bf16[1,384,128]{2,1,0:T(8,128)(2,1)S(1)} %collective-permute-done.3), channel_id=1, source_target_pairs={{0,4},{4,8},{8,12},{12,16},{16,20},{20,24},{24,28},{28,0},{1,5},{5... | collective-permute-start | bytes 294920 | tf_op jit(solution)/shard_map/ppermute | solution.py:17
  40.3 7.3 %collective-permute-start.5 = (bf16[1,384,128]{2,1,0:T(8,128)(2,1)S(1)}, bf16[1,384,128]{2,1,0:T(8,128)(2,1)S(1)}, u32[]{:S(2)}, u32[]{:S(2)}) collective-permute-start(bf16[1,384,128]{2,1,0:T(8,128)(2,1)S(1)} %collective-permute-done.4), channel_id=1, source_target_pairs={{0,4},{4,8},{8,12},{12,16},{16,20},{20,24},{24,28},{28,0},{1,5},{5... | collective-permute-start | bytes 294920 | tf_op jit(solution)/shard_map/ppermute | solution.py:17
  40.5 49.3 %copy-start.1 = (f32[512]{0:T(512)}, f32[512]{0:T(512)S(1)}, u32[]{:S(2)}) copy-start(f32[512]{0:T(512)S(1)} %get-tuple-element.228) | copy-start | bytes 6148
  47.6 8.1 %collective-permute-start.6 = (bf16[1,384,128]{2,1,0:T(8,128)(2,1)S(1)}, bf16[1,384,128]{2,1,0:T(8,128)(2,1)S(1)}, u32[]{:S(2)}, u32[]{:S(2)}) collective-permute-start(bf16[1,384,128]{2,1,0:T(8,128)(2,1)S(1)} %collective-permute-done.5), channel_id=1, source_target_pairs={{0,4},{4,8},{8,12},{12,16},{16,20},{20,24},{24,28},{28,0},{1,5},{5... | collective-permute-start | bytes 294920 | tf_op jit(solution)/shard_map/ppermute | solution.py:17
  55.8 32.8 %collective-permute-start.7 = (bf16[1,384,128]{2,1,0:T(8,128)(2,1)S(1)}, bf16[1,384,128]{2,1,0:T(8,128)(2,1)S(1)}, u32[]{:S(2)}, u32[]{:S(2)}) collective-permute-start(bf16[1,384,128]{2,1,0:T(8,128)(2,1)S(1)} %collective-permute-done.6), channel_id=1, source_target_pairs={{0,4},{4,8},{8,12},{12,16},{16,20},{20,24},{24,28},{28,0},{1,5},{5... | collective-permute-start | bytes 294920 | tf_op jit(solution)/shard_map/ppermute | solution.py:17
  122.4 89.0 %reduce-scatter.2.cloned.1.call-start = ((), (), s32[]{:S(2)}) async-start(), calls=%async_computation.2 | async-start | bytes 5242880 | tf_op jit(solution)/shard_map/reduce_scatter | solution.py:117
Sparse Core Ops, SparseCore 0:
  122.5 40.9 all-gather.1
  168.1 43.2 reduce-scatter.1
